TPU v7x, 32 devices: a whole 2x2x4 slice. The times are simulated.
32 devices in a mesh: tm: 4 (over x, core), space: 8 (over z, y).
Axes of the slice: x: 2, y: 2, z: 4, core: 2. Of those that a mesh axis runs over, the one named last changes fastest.
Arguments:
- starts: float32 [4, 32, 256, 384], P('tm', 'space'), may hold values from -18 to 18, as said below
- material: int32 [32, 256, 384], P('space'), may hold values from 0 to 7
- conductivity: float32 [8], replicated, may hold values from 0.3 to 3, as said below
Outputs:
- new_starts: float32 [4, 32, 256, 384], P('tm', 'space')
- coarse_path: float32 [4, 8, 64, 96], P('tm')
Inputs may be any that keep to these rules, and one draw needn't show every extreme that they name: `starts`: start states of order one. `conductivity`: positive conductivities.
All inputs are finite; a program needn't handle non-finite values.
Results may differ from a plain program's by a relative error of at most 0.0001.
Values sent between devices are 32-bit elements; how exact they have to be, the bound alone decides.
A program may use at most 128 MiB of HBM per device.

v0:
```python
import jax
import jax.numpy as jnp
from jax import lax
from jax.sharding import PartitionSpec as P

FACTOR = 4
SUBSTEPS = 2
SWEEPS = 2
JACOBI = 3


fine_step = 0.15
coarse_rate = 0.3
face_offsets = ((0, 1, 1), (2, 1, 1), (1, 0, 1), (1, 2, 1), (1, 1, 0), (1, 1, 2))


def extended(x, sides, width):
    for axis, dim in sides:
        peers, length = (lax.axis_size(axis), x.shape[dim])
        up = [(i, (i + 1) % peers) for i in range(peers - 1)]
        down = [(j, i) for i, j in up]
        last = lax.slice_in_dim(x, length - width, length, axis=dim)
        leading = lax.slice_in_dim(x, 0, width, axis=dim)
        before = lax.ppermute(last, axis, up)
        after = lax.ppermute(leading, axis, down)
        x = jnp.concatenate([before, x, after], axis=dim)
    return x


def shifted(x, axis, by):
    peers = lax.axis_size(axis)
    pairs = [(i, i + by) for i in range(peers) if 0 <= i + by < peers]
    return lax.ppermute(x, axis, pairs)


def window(padded, offsets, cells):
    return padded[
        offsets[0] : offsets[0] + cells[0],
        offsets[1] : offsets[1] + cells[1],
        offsets[2] : offsets[2] + cells[2],
    ]


def laplace_apply(padded, cells):
    summed = jnp.zeros(cells, jnp.float32)
    for shift_x in range(3):
        for shift_y in range(3):
            for shift_z in range(3):
                moved_axes = int(shift_x != 1) + int(shift_y != 1) + int(shift_z != 1)
                if moved_axes == 0:
                    continue
                weight = 0.5 ** (moved_axes - 1)
                summed = summed + weight * window(padded, (shift_x, shift_y, shift_z), cells)
    return 14.0 * window(padded, (1, 1, 1), cells) - summed


def operate(vector, root_cond):
    scaled = root_cond * vector
    padded = extended(scaled, (("space", 0),), 1)
    padded = jnp.pad(padded, ((0, 0), (1, 1), (1, 1)))
    return vector + fine_step * root_cond * laplace_apply(padded, vector.shape)


def grid_squares(resid):
    return lax.psum(jnp.sum(resid * resid), "space")


def grid_curvature(direction, image):
    return lax.psum(jnp.sum(direction * image), "space")


def substep(rhs_field, root_cond):
    iterate = rhs_field
    resid = rhs_field - operate(iterate, root_cond)
    direction = resid
    norm_now = grid_squares(resid)
    for sweep_index in range(SWEEPS):
        image = operate(direction, root_cond)
        step_len = norm_now / grid_curvature(direction, image)
        iterate = iterate + step_len * direction
        resid = resid - step_len * image
        if sweep_index + 1 < SWEEPS:
            norm_next = grid_squares(resid)
            direction = resid + norm_next / norm_now * direction
            norm_now = norm_next
    return iterate


def propagate(start_field, root_cond):
    current = start_field
    for step_index in range(SUBSTEPS):
        current = substep(current, root_cond)
    return current


def restrict(fine_field):
    size_x, size_y, size_z = fine_field.shape
    blocks = fine_field.reshape(
        size_x // FACTOR, FACTOR, size_y // FACTOR, FACTOR, size_z // FACTOR, FACTOR
    )
    return jnp.mean(blocks, axis=(1, 3, 5))


def prolong(coarse_field):
    size_x, size_y, size_z = coarse_field.shape
    spread = jnp.broadcast_to(
        coarse_field[:, None, :, None, :, None], (size_x, FACTOR, size_y, FACTOR, size_z, FACTOR)
    )
    return spread.reshape(size_x * FACTOR, size_y * FACTOR, size_z * FACTOR)


def coarse_setup(coarse_k):
    padded_k = jnp.pad(coarse_k, 1, mode="edge")
    face_coefs = []
    diagonal = jnp.ones(coarse_k.shape, jnp.float32)
    for offsets in face_offsets:
        coef = coarse_rate * 0.5 * (coarse_k + window(padded_k, offsets, coarse_k.shape))
        face_coefs.append(coef)
        diagonal = diagonal + coef
    return (face_coefs, diagonal)


def coarse_step(source, face_coefs, diagonal):
    iterate = source
    for sweep_index in range(JACOBI):
        padded = jnp.pad(iterate, 1)
        summed = jnp.zeros(source.shape, jnp.float32)
        for coef, offsets in zip(face_coefs, face_offsets):
            summed = summed + coef * window(padded, offsets, source.shape)
        iterate = (source + summed) / diagonal
    return iterate


def local(starts, material, conductivity):
    start_field = starts[0]
    conduct = jnp.zeros(start_field.shape, jnp.float32)
    for region in range(conductivity.shape[0]):
        conduct = conduct + jnp.where(material == region, conductivity[region], 0.0)
    root_cond = jnp.sqrt(conduct)
    coarse_start, coarse_k = (
        lax.all_gather(restrict(start_field), "space", axis=0, tiled=True),
        lax.all_gather(restrict(conduct), "space", axis=0, tiled=True),
    )
    face_coefs, diagonal = coarse_setup(coarse_k)
    coarse_old = coarse_step(coarse_start, face_coefs, diagonal)
    fine_end = propagate(start_field, root_cond)
    tm_index = lax.axis_index("tm")
    slice_count = lax.axis_size("tm")
    local_end = restrict(fine_end)
    coarse_end = lax.all_gather(local_end, "space", axis=0, tiled=True)
    jump_term = coarse_end - coarse_old
    coarse_rows = local_end.shape[0]
    carry_start = jnp.where(tm_index == 0, coarse_start, jnp.zeros_like(coarse_start))

    def relay_turn(turn_index, carry_in):
        stepped = coarse_step(carry_in, face_coefs, diagonal) + jump_term
        arrived = shifted(stepped, "tm", 1)
        return jnp.where(tm_index == turn_index + 1, arrived, carry_in)

    carry_own = lax.fori_loop(0, slice_count - 1, relay_turn, carry_start)
    path_own = coarse_step(carry_own, face_coefs, diagonal) + jump_term
    slab_offset = lax.axis_index("space") * coarse_rows
    path_slab = lax.dynamic_slice_in_dim(path_own, slab_offset, coarse_rows, 0)
    corrected = fine_end + prolong(path_slab - local_end)
    received = shifted(corrected, "tm", 1)
    new_field = jnp.where(tm_index == 0, start_field, received)
    return (new_field[None], path_own[None])


def solution(mesh):
    return jax.shard_map(
        local,
        mesh=mesh,
        in_specs=(P("tm", "space", None, None), P("space", None, None), P()),
        out_specs=(P("tm", "space", None, None), P("tm", None, None, None)),
        check_vma=False,
    )
```

profile of v0, /device:TPU:2, one launch (start us, length us, event | category | flops | bytes accessed | tf_op | source)
XLA Modules:
  0.0 589.5 jit_solution(5427695950292236274)
XLA Ops:
  0.6 1.6 fusion.298
  2.3 8.4 %bitcast_multiply_fusion = f32[4,256,384]{2,1,0:T(8,128)S(1)} fusion(f32[1,4,256,384]{3,2,1,0:T(8,128)} %param.5, f32[]{:T(128)} %bitcast.8, s32[4,256,384]{2,1,0:T(8,128)} %param.6, f32[]{:T(128)} %bitcast.7, f32[]{:T(128)} %bitcast.6, f32[]{:T(128)} %bitcast.5, f32[]{:T(128)} %bitcast.4, f32[]{:T(128)} %bitcast.3, f32[]{:T(128)} %bitcast.2, f32[]{:T(128)} %bitcast.1), kind=kLoop, calls=%fused_computation.382 | loop fusion | flops 9437184 | bytes 4718624 | tf_op jit(solution)/shard_map/mul | solution.py:58
  10.7 1.3 collective-permute-start.2
  12.0 4.6 collective-permute-start.1
  16.6 6.9 %collective-permute-done.2 = f32[1,256,384]{2,1,0:T(8,128)S(1)} collective-permute-done((f32[1,256,384]{2,1,0:T(8,128)S(1)}, f32[1,256,384]{2,1,0:T(8,128)S(1)}, u32[]{:S(2)}, u32[]{:S(2)}) %collective-permute-start.2) | collective-permute-done | bytes 393248 | tf_op jit(solution)/shard_map/ppermute | solution.py:25
  23.5 8.4 %collective-permute-done.1 = f32[1,256,384]{2,1,0:T(8,128)S(1)} collective-permute-done((f32[1,256,384]{2,1,0:T(8,128)S(1)}, f32[1,256,384]{2,1,0:T(8,128)S(1)}, u32[]{:S(2)}, u32[]{:S(2)}) %collective-permute-start.1) | collective-permute-done | bytes 393248 | tf_op jit(solution)/shard_map/ppermute | solution.py:24
  33.6 14.8 %sqrt_multiply_fusion.4 = (f32[4,256,384]{2,1,0:T(8,128)}, f32[4,256,384]{2,1,0:T(8,128)}) fusion(f32[]{:T(128)} %bitcast.8, s32[4,256,384]{2,1,0:T(8,128)} %param.6, f32[]{:T(128)} %bitcast.7, f32[]{:T(128)} %bitcast.6, f32[]{:T(128)} %bitcast.5, f32[]{:T(128)} %bitcast.4, f32[]{:T(128)} %bitcast.3, f32[]{:T(128)} %bitcast.2, f32[]{:T(128)} %bitcast.1, ...), kind=kLoop, calls=%fused_computation.402 | loop fusion | flops 30277632 | bytes 46399520 | tf_op jit(solution)/shard_map/mul | solution.py:58
  49.8 1.3 collective-permute-start.4
  51.1 5.0 collective-permute-start.3
  56.1 7.3 %collective-permute-done.4 = f32[1,256,384]{2,1,0:T(8,128)S(1)} collective-permute-done((f32[1,256,384]{2,1,0:T(8,128)S(1)}, f32[1,256,384]{2,1,0:T(8,128)S(1)}, u32[]{:S(2)}, u32[]{:S(2)}) %collective-permute-start.4) | collective-permute-done | bytes 393248 | tf_op jit(solution)/shard_map/ppermute | solution.py:25
  63.4 8.6 %collective-permute-done.3 = f32[1,256,384]{2,1,0:T(8,128)S(1)} collective-permute-done((f32[1,256,384]{2,1,0:T(8,128)S(1)}, f32[1,256,384]{2,1,0:T(8,128)S(1)}, u32[]{:S(2)}, u32[]{:S(2)}) %collective-permute-start.3) | collective-permute-done | bytes 393248 | tf_op jit(solution)/shard_map/ppermute | solution.py:24
  73.1 15.3 %multiply_reduce_fusion.4 = (f32[]{:T(128)}, f32[]{:T(128)}, f32[4,256,384]{2,1,0:T(8,128)}) fusion(f32[4,256,384]{2,1,0:T(8,128)} %get-tuple-element.313, f32[6,258,386]{2,1,0:T(8,128)S(1)} %select_maximum_fusion.8, f32[1,256,384]{2,1,0:T(8,128)} %copy-done.29, f32[4,256,384]{2,1,0:T(8,128)} %get-tuple-element.312, f32[1,256,384]{2,1,0:T(8,128)} %copy-done.32, ...), kind=kLoop, calls=%fused_computation.394 | loop fusion | flops 31064064 | bytes 44826664 | tf_op jit(solution)/shard_map/reduce_sum | solution.py:69
  88.3 20.4 %all-reduce.16 = (f32[]{:T(128)}, f32[]{:T(128)}) all-reduce(f32[]{:T(128)} %get-tuple-element.270, f32[]{:T(128)} %get-tuple-element.269), channel_id=1, replica_groups=mesh['tm'=4,'space'=8] {'space'}, use_global_device_ids=true, to_apply=%region_1.2 | all-reduce | flops 2 | bytes 16 | tf_op jit(solution)/shard_map/psum | solution.py:65
  110.1 3.0 multiply_reduce_fusion.3
  113.1 18.2 %psum.58 = f32[]{:T(128)} all-reduce(f32[]{:T(128)} %multiply_reduce_fusion.3), channel_id=1, replica_groups=mesh['tm'=4,'space'=8] {'space'}, use_global_device_ids=true, to_apply=%region_5.6 | all-reduce | flops 1 | bytes 8 | tf_op jit(solution)/shard_map/psum | solution.py:65
  132.6 8.1 %sqrt_multiply_fusion.3 = f32[4,256,384]{2,1,0:T(8,128)S(1)} fusion(f32[4,256,384]{2,1,0:T(8,128)S(1)} %copy-done.13, f32[]{:T(128)S(6)} %div.82, f32[4,256,384]{2,1,0:T(8,128)} %get-tuple-element.311, f32[]{:T(128)S(6)} %div.81, f32[]{:T(128)} %bitcast.8, s32[4,256,384]{2,1,0:T(8,128)S(1)} %copy-done, f32[]{:T(128)} %bitcast.7, f32[]{:T(128)} %bitcast.6, ...), kind=kLoop, calls=%fused_computation.401 | loop fusion | flops 11010048 | bytes 6291496 | tf_op jit(solution)/shard_map/mul | solution.py:58
  140.8 1.3 collective-permute-start.6
  142.1 4.6 collective-permute-start.5
  146.7 3.8 collective-permute-done.6
  150.5 5.1 collective-permute-done.5
  157.3 14.7 %fusion.43 = f32[]{:T(128)} fusion(f32[6,258,386]{2,1,0:T(8,128)S(1)} %select_maximum_fusion.6, f32[1,256,384]{2,1,0:T(8,128)} %copy-done.33, f32[4,256,384]{2,1,0:T(8,128)} %copy-done.23, f32[1,256,384]{2,1,0:T(8,128)} %copy-done.36, f32[4,256,384]{2,1,0:T(8,128)} %get-tuple-element.313, f32[]{:T(128)S(6)} %div.82, f32[4,256,384]{2,1,0:T(8,128)} %get-tuple-element.311, ...), kind=kLoop, calls=%fused_computation.82 | loop fusion | flops 31850496 | bytes 44826668 | tf_op jit(solution)/shard_map/reduce_sum | solution.py:69
  172.0 20.2 %psum.59 = f32[]{:T(128)} all-reduce(f32[]{:T(128)} %fusion.43), channel_id=1, replica_groups=mesh['tm'=4,'space'=8] {'space'}, use_global_device_ids=true, to_apply=%region_7.8 | all-reduce | flops 1 | bytes 8 | tf_op jit(solution)/shard_map/psum | solution.py:69
  193.6 10.9 %sqrt_multiply_fusion.2 = (f32[4,256,384]{2,1,0:T(8,128)S(1)}, f32[4,256,384]{2,1,0:T(8,128)}) fusion(f32[]{:T(128)} %bitcast.8, s32[4,256,384]{2,1,0:T(8,128)} %param.6, f32[]{:T(128)} %bitcast.7, f32[]{:T(128)} %bitcast.6, f32[]{:T(128)} %bitcast.5, f32[]{:T(128)} %bitcast.4, f32[]{:T(128)} %bitcast.3, f32[]{:T(128)} %bitcast.2, f32[]{:T(128)} %bitcast.1, ...), kind=kLoop, calls=%fused_computation.400 | loop fusion | flops 12582912 | bytes 9437228 | tf_op jit(solution)/shard_map/mul | solution.py:58
  204.5 1.3 collective-permute-start.8
  205.8 4.7 collective-permute-start.7
  210.6 3.6 collective-permute-done.8
  214.2 2.2 collective-permute-done.7
  217.4 14.9 %sqrt_multiply_fusion.1 = (f32[4,256,384]{2,1,0:T(8,128)}, f32[4,256,384]{2,1,0:T(8,128)}) fusion(f32[]{:T(128)} %bitcast.8, s32[4,256,384]{2,1,0:T(8,128)} %param.6, f32[]{:T(128)} %bitcast.7, f32[]{:T(128)} %bitcast.6, f32[]{:T(128)} %bitcast.5, f32[]{:T(128)} %bitcast.4, f32[]{:T(128)} %bitcast.3, f32[]{:T(128)} %bitcast.2, f32[]{:T(128)} %bitcast.1, ...), kind=kLoop, calls=%fused_computation.399 | loop fusion | flops 30277632 | bytes 46399520 | tf_op jit(solution)/shard_map/mul | solution.py:58
  233.6 1.3 collective-permute-start.10
  234.9 5.8 collective-permute-start.9
  240.7 14.7 %reduce_sum.129 = f32[64,4,96,4]{3,2,1,0:T(8,128)} reshape(f32[256,384]{1,0:T(8,128)S(1)} %reduce_sum.128) | data formatting | bytes 786432 | tf_op jit(solution)/shard_map/reduce_sum | solution.py:101
  255.4 5.7 reduce_sum.130
  261.2 30.8 %all-gather = f32[512,96]{1,0:T(8,128)S(1)} all-gather(f32[64,96]{1,0:T(8,128)S(1)} %broadcast_multiply_fusion.2), channel_id=2, replica_groups=mesh['tm'=4,'space'=8] {'space'}, dimensions={0}, use_global_device_ids=true | all-gather | bytes 221184 | tf_op jit(solution)/shard_map/all_gather | solution.py:141
  292.8 2.6 select_maximum_fusion.2
  295.3 15.3 %multiply_reduce_fusion.1 = (f32[]{:T(128)}, f32[]{:T(128)}, f32[4,256,384]{2,1,0:T(8,128)}) fusion(f32[4,256,384]{2,1,0:T(8,128)} %get-tuple-element.308, f32[6,258,386]{2,1,0:T(8,128)S(1)} %select_maximum_fusion.2, f32[1,256,384]{2,1,0:T(8,128)} %copy-done.28, f32[4,256,384]{2,1,0:T(8,128)} %get-tuple-element.307, ...), kind=kLoop, calls=%fused_computation.389 | loop fusion | flops 31064064 | bytes 44826664 | tf_op jit(solution)/shard_map/reduce_sum | solution.py:69
  310.7 19.9 %all-reduce.15 = (f32[]{:T(128)}, f32[]{:T(128)}) all-reduce(f32[]{:T(128)} %get-tuple-element.268, f32[]{:T(128)} %get-tuple-element.267), channel_id=1, replica_groups=mesh['tm'=4,'space'=8] {'space'}, use_global_device_ids=true, to_apply=%region_9.10 | all-reduce | flops 2 | bytes 16 | tf_op jit(solution)/shard_map/psum | solution.py:65
  331.9 3.1 multiply_reduce_fusion
  335.0 18.0 %psum.62 = f32[]{:T(128)} all-reduce(f32[]{:T(128)} %multiply_reduce_fusion), channel_id=1, replica_groups=mesh['tm'=4,'space'=8] {'space'}, use_global_device_ids=true, to_apply=%region_13.14 | all-reduce | flops 1 | bytes 8 | tf_op jit(solution)/shard_map/psum | solution.py:65
  354.3 9.0 %fusion.280 = (f32[256,384]{1,0:T(8,128)}, f32[4,256,384]{2,1,0:T(8,128)S(1)}) fusion(f32[]{:T(128)} %bitcast.8, s32[4,256,384]{2,1,0:T(8,128)S(1)} %copy-done.1, f32[]{:T(128)} %bitcast.7, f32[]{:T(128)} %bitcast.6, f32[]{:T(128)} %bitcast.5, f32[]{:T(128)} %bitcast.4, f32[]{:T(128)} %bitcast.3, f32[]{:T(128)} %bitcast.2, f32[]{:T(128)} %bitcast.1, ...), kind=kLoop, calls=%fused_computation.563 | loop fusion | flops 11304960 | bytes 6684712 | tf_op jit(solution)/shard_map/reduce_sum | solution.py:101
  364.4 1.3 collective-permute-start.12
  365.7 5.6 collective-permute-start.11
  371.3 14.6 %reduce_sum.132 = f32[64,4,96,4]{3,2,1,0:T(8,128)} reshape(f32[256,384]{1,0:T(8,128)S(1)} %copy-done.37) | data formatting | bytes 786432 | tf_op jit(solution)/shard_map/reduce_sum | solution.py:101
  385.9 5.7 reduce_sum.133
  391.7 30.7 %all-gather.1 = f32[512,96]{1,0:T(8,128)S(1)} all-gather(f32[64,96]{1,0:T(8,128)S(1)} %broadcast_multiply_fusion.1), channel_id=3, replica_groups=mesh['tm'=4,'space'=8] {'space'}, dimensions={0}, use_global_device_ids=true | all-gather | bytes 221184 | tf_op jit(solution)/shard_map/all_gather | solution.py:142
  425.8 2.1 select_maximum_fusion
  427.9 14.7 %fusion.44 = f32[]{:T(128)} fusion(f32[6,258,386]{2,1,0:T(8,128)S(1)} %select_maximum_fusion, f32[1,256,384]{2,1,0:T(8,128)} %copy-done.27, f32[4,256,384]{2,1,0:T(8,128)} %copy-done.20, f32[1,256,384]{2,1,0:T(8,128)} %collective-permute-done.11, f32[4,256,384]{2,1,0:T(8,128)} %get-tuple-element.308, f32[]{:T(128)S(6)} %div.85, ...), kind=kLoop, calls=%fused_computation.83 | loop fusion | flops 31850496 | bytes 44826668 | tf_op jit(solution)/shard_map/reduce_sum | solution.py:69
  442.6 2.4 broadcast_select_fusion.1
  445.0 20.1 %psum.63 = f32[]{:T(128)} all-reduce(f32[]{:T(128)} %fusion.44), channel_id=1, replica_groups=mesh['tm'=4,'space'=8] {'space'}, use_global_device_ids=true, to_apply=%region_15.16 | all-reduce | flops 1 | bytes 8 | tf_op jit(solution)/shard_map/psum | solution.py:69
  466.4 3.5 fusion.287
  470.0 14.6 %reduce_sum.135 = f32[64,4,96,4]{3,2,1,0:T(8,128)} reshape(f32[256,384]{1,0:T(8,128)S(1)} %get-tuple-element.304) | data formatting | bytes 786432 | tf_op jit(solution)/shard_map/reduce_sum | solution.py:101
  484.6 5.8 reduce_sum.136
  490.5 30.9 %all-gather.2 = f32[512,96]{1,0:T(8,128)S(1)} all-gather(f32[64,96]{1,0:T(8,128)S(1)} %broadcast_multiply_fusion), channel_id=4, replica_groups=mesh['tm'=4,'space'=8] {'space'}, dimensions={0}, use_global_device_ids=true | all-gather | bytes 221184 | tf_op jit(solution)/shard_map/all_gather | solution.py:150
  521.7 25.7 %while.15 = (s32[]{:T(128)}, f32[8,64,96]{2,1,0:T(8,128)S(1)}, s32[]{:T(128)}, f32[8,64,96]{2,1,0:T(8,128)S(1)}, f32[8,64,96]{2,1,0:T(8,128)S(1)}, /*index=5*/f3...) while((s32[]{:T(128)}, f32[8,64,96]{2,1,0:T(8,128)S(1)}, ...), condition=%wide.region_23.24_spmd, body=%wide.region_22.23_spmd.sunk | while | flops 2015235 | bytes 7274663 | solution.py:160
  522.6 1.9 collective-permute-start
  524.5 5.8 collective-permute-done
  531.1 1.9 collective-permute-start
  533.1 5.8 collective-permute-done
  539.7 1.9 collective-permute-start
  541.6 5.8 collective-permute-done
  548.4 5.5 broadcast_in_dim.72
  553.9 11.8 %broadcast_in_dim.73 = f32[256,384]{1,0:T(8,128)S(1)} reshape(f32[64,4,96,4]{3,2,1,0:T(8,128)} %broadcast_in_dim.72) | data formatting | bytes 786432 | tf_op jit(solution)/shard_map/broadcast_in_dim | solution.py:106
  565.9 2.1 collective-permute-start.13
  567.9 19.8 %collective-permute-done.13 = f32[4,256,384]{2,1,0:T(8,128)S(1)} collective-permute-done((f32[4,256,384]{2,1,0:T(8,128)S(1)}, f32[4,256,384]{2,1,0:T(8,128)S(1)}, u32[]{:S(2)}, u32[]{:S(2)}) %collective-permute-start.13) | collective-permute-done | bytes 1572896 | tf_op jit(solution)/shard_map/ppermute | solution.py:33
  587.7 1.3 fusion.185
  (120 shorter events, 17.6 us)
Async XLA Ops:
  10.7 21.2 %copy-start.22 = (f32[4,256,384]{2,1,0:T(8,128)}, f32[4,256,384]{2,1,0:T(8,128)S(1)}, u32[]{:S(2)}) copy-start(f32[4,256,384]{2,1,0:T(8,128)S(1)} %bitcast_multiply_fusion) | copy-start | bytes 4718596
  10.7 12.7 %collective-permute-start.2 = (f32[1,256,384]{2,1,0:T(8,128)S(1)}, f32[1,256,384]{2,1,0:T(8,128)S(1)}, u32[]{:S(2)}, u32[]{:S(2)}) collective-permute-start(f32[1,256,384]{2,1,0:T(8,128)S(1)} %get-tuple-element.327), channel_id=1, source_target_pairs={{1,0},{2,1},{3,2},{4,3},{5,4},{6,5},{7,6},{9,8},{10,9},{11,10},{12... | collective-permute-start | bytes 1179656 | tf_op jit(solution)/shard_map/ppermute | solution.py:25
  12.0 19.8 %collective-permute-start.1 = (f32[1,256,384]{2,1,0:T(8,128)S(1)}, f32[1,256,384]{2,1,0:T(8,128)S(1)}, u32[]{:S(2)}, u32[]{:S(2)}) collective-permute-start(f32[1,256,384]{2,1,0:T(8,128)S(1)} %get-tuple-element.326), channel_id=1, source_target_pairs={{0,1},{1,2},{2,3},{3,4},{4,5},{5,6},{6,7},{8,9},{9,10},{10,11},{11... | collective-permute-start | bytes 1179656 | tf_op jit(solution)/shard_map/ppermute | solution.py:24
  23.5 8.4 %copy-start.31 = (f32[1,256,384]{2,1,0:T(8,128)}, f32[1,256,384]{2,1,0:T(8,128)S(1)}, u32[]{:S(2)}) copy-start(f32[1,256,384]{2,1,0:T(8,128)S(1)} %collective-permute-done.2) | copy-start | bytes 1179652
  31.8 0.8 copy-start.35
  48.5 23.5 %copy-start.18 = (f32[4,256,384]{2,1,0:T(8,128)S(1)}, f32[4,256,384]{2,1,0:T(8,128)}, u32[]{:S(2)}) copy-start(f32[4,256,384]{2,1,0:T(8,128)} %get-tuple-element.312) | copy-start | bytes 4718596
  49.8 13.7 %collective-permute-start.4 = (f32[1,256,384]{2,1,0:T(8,128)S(1)}, f32[1,256,384]{2,1,0:T(8,128)S(1)}, u32[]{:S(2)}, u32[]{:S(2)}) collective-permute-start(f32[1,256,384]{2,1,0:T(8,128)S(1)} %get-tuple-element.325), channel_id=1, source_target_pairs={{1,0},{2,1},{3,2},{4,3},{5,4},{6,5},{7,6},{9,8},{10,9},{11,10},{12... | collective-permute-start | bytes 1179656 | tf_op jit(solution)/shard_map/ppermute | solution.py:25
  51.1 21.0 %collective-permute-start.3 = (f32[1,256,384]{2,1,0:T(8,128)S(1)}, f32[1,256,384]{2,1,0:T(8,128)S(1)}, u32[]{:S(2)}, u32[]{:S(2)}) collective-permute-start(f32[1,256,384]{2,1,0:T(8,128)S(1)} %get-tuple-element.324), channel_id=1, source_target_pairs={{0,1},{1,2},{2,3},{3,4},{4,5},{5,6},{6,7},{8,9},{9,10},{10,11},{11... | collective-permute-start | bytes 1179656 | tf_op jit(solution)/shard_map/ppermute | solution.py:24
  63.4 9.6 %copy-start.29 = (f32[1,256,384]{2,1,0:T(8,128)}, f32[1,256,384]{2,1,0:T(8,128)S(1)}, u32[]{:S(2)}) copy-start(f32[1,256,384]{2,1,0:T(8,128)S(1)} %collective-permute-done.4) | copy-start | bytes 1179652
  72.0 1.0 copy-start.32
  110.0 22.5 %copy-start = (s32[4,256,384]{2,1,0:T(8,128)S(1)}, s32[4,256,384]{2,1,0:T(8,128)}, u32[]{:S(2)}) copy-start(s32[4,256,384]{2,1,0:T(8,128)} %param.6) | copy-start | bytes 4718596
  110.0 22.5 %copy-start.13 = (f32[4,256,384]{2,1,0:T(8,128)S(1)}, f32[4,256,384]{2,1,0:T(8,128)}, u32[]{:S(2)}) copy-start(f32[4,256,384]{2,1,0:T(8,128)} %get-tuple-element.313) | copy-start | bytes 4718596
  140.7 14.8 %copy-start.23 = (f32[4,256,384]{2,1,0:T(8,128)}, f32[4,256,384]{2,1,0:T(8,128)S(1)}, u32[]{:S(2)}) copy-start(f32[4,256,384]{2,1,0:T(8,128)S(1)} %sqrt_multiply_fusion.3) | copy-start | bytes 4718596
  140.8 9.7 %collective-permute-start.6 = (f32[1,256,384]{2,1,0:T(8,128)S(1)}, f32[1,256,384]{2,1,0:T(8,128)S(1)}, u32[]{:S(2)}, u32[]{:S(2)}) collective-permute-start(f32[1,256,384]{2,1,0:T(8,128)S(1)} %get-tuple-element.323), channel_id=1, source_target_pairs={{1,0},{2,1},{3,2},{4,3},{5,4},{6,5},{7,6},{9,8},{10,9},{11,10},{12... | collective-permute-start | bytes 1179656 | tf_op jit(solution)/shard_map/ppermute | solution.py:25
  142.1 13.4 %collective-permute-start.5 = (f32[1,256,384]{2,1,0:T(8,128)S(1)}, f32[1,256,384]{2,1,0:T(8,128)S(1)}, u32[]{:S(2)}, u32[]{:S(2)}) collective-permute-start(f32[1,256,384]{2,1,0:T(8,128)S(1)} %get-tuple-element.322), channel_id=1, source_target_pairs={{0,1},{1,2},{2,3},{3,4},{4,5},{5,6},{6,7},{8,9},{9,10},{10,11},{11... | collective-permute-start | bytes 1179656 | tf_op jit(solution)/shard_map/ppermute | solution.py:24
  150.5 5.1 copy-start.33
  155.5 0.8 copy-start.36
  204.5 12.9 %copy-start.19 = (f32[4,256,384]{2,1,0:T(8,128)}, f32[4,256,384]{2,1,0:T(8,128)S(1)}, u32[]{:S(2)}) copy-start(f32[4,256,384]{2,1,0:T(8,128)S(1)} %get-tuple-element.309) | copy-start | bytes 4718596
  204.5 9.7 %collective-permute-start.8 = (f32[1,256,384]{2,1,0:T(8,128)S(1)}, f32[1,256,384]{2,1,0:T(8,128)S(1)}, u32[]{:S(2)}, u32[]{:S(2)}) collective-permute-start(f32[1,256,384]{2,1,0:T(8,128)S(1)} %get-tuple-element.321), channel_id=1, source_target_pairs={{1,0},{2,1},{3,2},{4,3},{5,4},{6,5},{7,6},{9,8},{10,9},{11,10},{12... | collective-permute-start | bytes 1179656 | tf_op jit(solution)/shard_map/ppermute | solution.py:25
  205.8 10.5 %collective-permute-start.7 = (f32[1,256,384]{2,1,0:T(8,128)S(1)}, f32[1,256,384]{2,1,0:T(8,128)S(1)}, u32[]{:S(2)}, u32[]{:S(2)}) collective-permute-start(f32[1,256,384]{2,1,0:T(8,128)S(1)} %get-tuple-element.320), channel_id=1, source_target_pairs={{0,1},{1,2},{2,3},{3,4},{4,5},{5,6},{6,7},{8,9},{9,10},{10,11},{11... | collective-permute-start | bytes 1179656 | tf_op jit(solution)/shard_map/ppermute | solution.py:24
  214.2 3.2 copy-start.30
  216.4 1.0 copy-start.34
  232.3 8.4 %copy-start.16 = (f32[1,4,256,384]{3,2,1,0:T(8,128)S(1)}, f32[1,4,256,384]{3,2,1,0:T(8,128)}, u32[]{:S(2)}) copy-start(f32[1,4,256,384]{3,2,1,0:T(8,128)} %param.5) | copy-start | bytes 4718596
  233.6 58.4 %collective-permute-start.10 = (f32[1,256,384]{2,1,0:T(8,128)S(1)}, f32[1,256,384]{2,1,0:T(8,128)S(1)}, u32[]{:S(2)}, u32[]{:S(2)}) collective-permute-start(f32[1,256,384]{2,1,0:T(8,128)S(1)} %get-tuple-element.319), channel_id=1, source_target_pairs={{1,0},{2,1},{3,2},{4,3},{5,4},{6,5},{7,6},{9,8},{10,9},{11,10},{12... | collective-permute-start | bytes 1179656 | tf_op jit(solution)/shard_map/ppermute | solution.py:25
  234.9 57.9 %collective-permute-start.9 = (f32[1,256,384]{2,1,0:T(8,128)S(1)}, f32[1,256,384]{2,1,0:T(8,128)}, u32[]{:S(2)}, u32[]{:S(2)}) collective-permute-start(f32[1,256,384]{2,1,0:T(8,128)S(1)} %get-tuple-element.318), channel_id=1, source_target_pairs={{0,1},{1,2},{2,3},{3,4},{4,5},{5,6},{6,7},{8,9},{9,10},{10,11},{11... | collective-permute-start | bytes 1179656 | tf_op jit(solution)/shard_map/ppermute | solution.py:24
  292.0 131.8 %copy-start.25 = (f32[512,96]{1,0:T(8,128)}, f32[512,96]{1,0:T(8,128)S(1)}, u32[]{:S(2)}) copy-start(f32[512,96]{1,0:T(8,128)S(1)} %all-gather) | copy-start | bytes 589828
  292.0 0.8 copy-start.28
  331.9 22.4 %copy-start.1 = (s32[4,256,384]{2,1,0:T(8,128)S(1)}, s32[4,256,384]{2,1,0:T(8,128)}, u32[]{:S(2)}) copy-start(s32[4,256,384]{2,1,0:T(8,128)} %param.6) | copy-start | bytes 4718596
  331.9 22.4 %copy-start.14 = (f32[4,256,384]{2,1,0:T(8,128)S(1)}, f32[4,256,384]{2,1,0:T(8,128)}, u32[]{:S(2)}) copy-start(f32[4,256,384]{2,1,0:T(8,128)} %get-tuple-element.308) | copy-start | bytes 4718596
  363.2 1.1 copy-start.20
  363.2 8.1 %copy-start.37 = (f32[256,384]{1,0:T(8,128)S(1)}, f32[256,384]{1,0:T(8,128)}, u32[]{:S(2)}) copy-start(f32[256,384]{1,0:T(8,128)} %get-tuple-element.314) | copy-start | bytes 1179652
  364.4 60.4 %collective-permute-start.12 = (f32[1,256,384]{2,1,0:T(8,128)S(1)}, f32[1,256,384]{2,1,0:T(8,128)S(1)}, u32[]{:S(2)}, u32[]{:S(2)}) collective-permute-start(f32[1,256,384]{2,1,0:T(8,128)S(1)} %get-tuple-element.317), channel_id=1, source_target_pairs={{1,0},{2,1},{3,2},{4,3},{5,4},{6,5},{7,6},{9,8},{10,9},{11,10},{12... | collective-permute-start | bytes 1179656 | tf_op jit(solution)/shard_map/ppermute | solution.py:25
  365.7 59.9 %collective-permute-start.11 = (f32[1,256,384]{2,1,0:T(8,128)S(1)}, f32[1,256,384]{2,1,0:T(8,128)}, u32[]{:S(2)}, u32[]{:S(2)}) collective-permute-start(f32[1,256,384]{2,1,0:T(8,128)S(1)} %get-tuple-element.316), channel_id=1, source_target_pairs={{0,1},{1,2},{2,3},{3,4},{4,5},{5,6},{6,7},{8,9},{9,10},{10,11},{11... | collective-permute-start | bytes 1179656 | tf_op jit(solution)/shard_map/ppermute | solution.py:24
  423.8 1.0 copy-start.2
  423.8 1.0 copy-start.4
  423.8 1.0 copy-start.6
  423.8 1.1 copy-start.8
  423.8 1.1 copy-start.10
  423.8 2.0 copy-start.21
  424.9 0.7 copy-start.27
  442.6 23.8 %copy-start.15 = (f32[4,256,384]{2,1,0:T(8,128)S(1)}, f32[4,256,384]{2,1,0:T(8,128)}, u32[]{:S(2)}) copy-start(f32[4,256,384]{2,1,0:T(8,128)} %get-tuple-element.308) | copy-start | bytes 4718596
  484.6 36.8 %copy-start.3 = (f32[8,64,96]{2,1,0:T(8,128)S(1)}, f32[8,64,96]{2,1,0:T(8,128)}, u32[]{:S(2)}) copy-start(f32[8,64,96]{2,1,0:T(8,128)} %copy-done.2) | copy-start | bytes 589828
  484.6 36.8 %copy-start.5 = (f32[8,64,96]{2,1,0:T(8,128)S(1)}, f32[8,64,96]{2,1,0:T(8,128)}, u32[]{:S(2)}) copy-start(f32[8,64,96]{2,1,0:T(8,128)} %copy-done.4) | copy-start | bytes 589828
  484.6 36.8 %copy-start.7 = (f32[8,64,96]{2,1,0:T(8,128)S(1)}, f32[8,64,96]{2,1,0:T(8,128)}, u32[]{:S(2)}) copy-start(f32[8,64,96]{2,1,0:T(8,128)} %copy-done.6) | copy-start | bytes 589828
  484.6 36.8 %copy-start.9 = (f32[8,64,96]{2,1,0:T(8,128)S(1)}, f32[8,64,96]{2,1,0:T(8,128)}, u32[]{:S(2)}) copy-start(f32[8,64,96]{2,1,0:T(8,128)} %copy-done.8) | copy-start | bytes 589828
  484.6 36.8 %copy-start.11 = (f32[8,64,96]{2,1,0:T(8,128)S(1)}, f32[8,64,96]{2,1,0:T(8,128)}, u32[]{:S(2)}) copy-start(f32[8,64,96]{2,1,0:T(8,128)} %copy-done.10) | copy-start | bytes 589828
  484.6 36.8 %copy-start.26 = (f32[512,96]{1,0:T(8,128)S(1)}, f32[512,96]{1,0:T(8,128)}, u32[]{:S(2)}) copy-start(f32[512,96]{1,0:T(8,128)} %copy-done.25) | copy-start | bytes 589828
  490.5 31.2 %copy-start.12 = (f32[8,64,96]{2,1,0:T(8,128)S(1)}, f32[8,64,96]{2,1,0:T(8,128)}, u32[]{:S(2)}) copy-start(f32[8,64,96]{2,1,0:T(8,128)} %get-tuple-element.420) | copy-start | bytes 589828
  522.6 7.7 %collective-permute-start = (f32[8,64,96]{2,1,0:T(8,128)S(1)}, f32[8,64,96]{2,1,0:T(8,128)S(1)}, u32[]{:S(2)}, u32[]{:S(2)}) collective-permute-start(f32[8,64,96]{2,1,0:T(8,128)S(1)} %fusion.304), channel_id=1, source_target_pairs={{0,8},{8,16},{16,24},{1,9},{9,17},{17,25},{2,10},{10,18},{18,26},{... | collective-permute-start | bytes 589832 | tf_op jit(solution)/shard_map/while/body/eval_jaxpr/ppermute | solution.py:33
  531.1 7.7 %collective-permute-start = (f32[8,64,96]{2,1,0:T(8,128)S(1)}, f32[8,64,96]{2,1,0:T(8,128)S(1)}, u32[]{:S(2)}, u32[]{:S(2)}) collective-permute-start(f32[8,64,96]{2,1,0:T(8,128)S(1)} %fusion.304), channel_id=1, source_target_pairs={{0,8},{8,16},{16,24},{1,9},{9,17},{17,25},{2,10},{10,18},{18,26},{... | collective-permute-start | bytes 589832 | tf_op jit(solution)/shard_map/while/body/eval_jaxpr/ppermute | solution.py:33
  539.7 7.7 %collective-permute-start = (f32[8,64,96]{2,1,0:T(8,128)S(1)}, f32[8,64,96]{2,1,0:T(8,128)S(1)}, u32[]{:S(2)}, u32[]{:S(2)}) collective-permute-start(f32[8,64,96]{2,1,0:T(8,128)S(1)} %fusion.304), channel_id=1, source_target_pairs={{0,8},{8,16},{16,24},{1,9},{9,17},{17,25},{2,10},{10,18},{18,26},{... | collective-permute-start | bytes 589832 | tf_op jit(solution)/shard_map/while/body/eval_jaxpr/ppermute | solution.py:33
  548.4 5.6 copy-start.38
  553.9 11.8 %copy-start.24 = (f32[4,256,384]{2,1,0:T(8,128)S(1)}, f32[4,256,384]{2,1,0:T(8,128)}, u32[]{:S(2)}) copy-start(f32[4,256,384]{2,1,0:T(8,128)} %get-tuple-element.305) | copy-start | bytes 4718596
  565.7 22.0 %copy-start.17 = (f32[1,4,256,384]{3,2,1,0:T(8,128)S(1)}, f32[1,4,256,384]{3,2,1,0:T(8,128)}, u32[]{:S(2)}) copy-start(f32[1,4,256,384]{3,2,1,0:T(8,128)} %param.5) | copy-start | bytes 4718596
  565.9 21.9 %collective-permute-start.13 = (f32[4,256,384]{2,1,0:T(8,128)S(1)}, f32[4,256,384]{2,1,0:T(8,128)S(1)}, u32[]{:S(2)}, u32[]{:S(2)}) collective-permute-start(f32[4,256,384]{2,1,0:T(8,128)S(1)} %broadcast_add_fusion), channel_id=1, source_target_pairs={{0,8},{8,16},{16,24},{1,9},{9,17},{17,25},{2,10},{10,18},{18,26},{... | collective-permute-start | bytes 4718600 | tf_op jit(solution)/shard_map/ppermute | solution.py:33
where the time goes:
time: 598 us; the launch traced here: 589 us
  blocking collectives  209 us (35%)
  other arithmetic  172 us (29%)
  waiting for transfers between devices  82.8 us (14%)
  local copies, waits for them, and re-layouts  70.3 us (12%)
  starting transfers between devices  45.8 us (8%)
  between operations  9.37 us (2%)
    psum x4, blocking collectives, grid_squares(): return lax.psum(jnp.sum(resid * resid), 'space')  76.6 us
    reduce_sum x4, other arithmetic, grid_curvature(): return lax.psum(jnp.sum(direction * image), 'space')  60.1 us
    mul x5, other arithmetic, operate(): scaled = root_cond * vector  57.2 us
    reduce_sum x3, local copies, waits for them, and re-layouts, restrict(): return jnp.mean(blocks, axis=(1, 3, 5))  43.9 us
    psum x2, blocking collectives, grid_curvature(): return lax.psum(jnp.sum(direction * image), 'space')  40.3 us
    ppermute x4, waiting for transfers between devices, shifted(): return lax.ppermute(x, axis, pairs)  37.1 us
    all_gather x1, blocking collectives, local(): coarse_end = lax.all_gather(local_end, 'space', axis=0, tiled=True)  30.9 us
    all_gather x1, blocking collectives, local(): lax.all_gather(restrict(start_field), 'space', axis=0, tiled=True)  30.8 us
  transfers between devices with their start and end apart: 16, of which 12 were waited for; matrix products, arithmetic and copies ran while one was open for 7% of the time, Pallas kernels for 0%

commit v1 on v0

v1 whole, which is shorter than its diff:
```python
import functools

import jax
import jax.numpy as jnp
from jax import lax
from jax.experimental import pallas as pl
from jax.experimental.pallas import tpu as pltpu
from jax.sharding import PartitionSpec as P

FACTOR = 4
JACOBI = 3
W = 5
RH = 8
LANES = 128
HIGH = lax.Precision.HIGHEST
MESH = pl.DeviceIdType.MESH


def quarter(shape, long_axis):
    fine = lax.shift_right_logical(lax.broadcasted_iota(jnp.int32, shape, long_axis), 2)
    coarse = lax.broadcasted_iota(jnp.int32, shape, 1 - long_axis)
    return jnp.where(fine == coarse, 1.0, 0.0).astype(jnp.float32)


def mm(a, b):
    return jnp.dot(a, b, precision=HIGH, preferred_element_type=jnp.float32)


def kernel(
    T, S, L, NY, NZ, regions,
    cond_ref, st_ref, mat_ref,
    out_ref, path_ref,
    k_slab, b, k, ua, ub, r, q, xf, fe,
    red, gath, ce, pin, din, dsend, coefs, rdiag,
    b_recv, k_recv, b_ysend, k_ysend, b_zsend, k_zsend, k_sib,
    a_send, a_recv, g_send, g_recv, c_send, c_recv, e_send, e_recv, p_send, p_recv,
):
    tm = lax.axis_index("tm")
    s = lax.axis_index("space")
    h = lax.rem(s, 2)
    p = s // 2
    NP = S // 2
    PL = 2 * L
    E = PL + 2 * W
    HY = NY // 2
    RW = HY + RH
    RE = HY + 2 * RH
    partner = s + 1 - 2 * h
    par = lax.rem(tm, 2)
    sib = tm + 1 - 2 * par
    has_up = p < NP - 1
    has_dn = p > 0
    LC = L // FACTOR
    XC = LC * S
    YC = NY // FACTOR
    ZC = NZ // FACTOR

    def dev(t_, s_):
        return (t_, s_)

    def remote(src, dst, ss, rs, d):
        return pltpu.make_async_remote_copy(
            src_ref=src, dst_ref=dst, send_sem=ss, recv_sem=rs, device_id=d, device_id_type=MESH
        )

    own_off = pl.multiple_of(RH - RH * h, 8)
    own_src = pl.multiple_of((HY - RH) * h, 8)
    oth_off = pl.multiple_of(RH * h, 8)
    oth_src = pl.multiple_of((HY - RH) * (1 - h), 8)
    own_rows = pl.ds(own_off, RW)
    zero_rows = pl.ds(pl.multiple_of(h * RW, 8), RH)

    bar = pltpu.get_barrier_semaphore()
    for i in range(1, S):
        pl.semaphore_signal(bar, 1, device_id=dev(tm, lax.rem(s + i, S)), device_id_type=MESH)

    @pl.when(tm < T - 1)
    def _():
        pl.semaphore_signal(bar, 1, device_id=dev(tm + 1, s), device_id_type=MESH)
        pl.semaphore_signal(bar, 1, device_id=dev(tm + 1, partner), device_id_type=MESH)

    @pl.when(tm > 0)
    def _():
        pl.semaphore_signal(bar, 1, device_id=dev(tm - 1, s), device_id_type=MESH)
        pl.semaphore_signal(bar, 1, device_id=dev(tm - 1, partner), device_id_type=MESH)

    tm_peers = 2 * jnp.where(tm < T - 1, 1, 0) + 2 * jnp.where(tm > 0, 1, 0)
    pl.semaphore_wait(bar, S - 1 + tm_peers)

    def y_copy(slab, ext, t, ss, rs):
        e = W + h * L + t
        return remote(
            slab.at[t, pl.ds(oth_src, RW), :], ext.at[e, pl.ds(oth_off, RW), :],
            ss.at[t], rs.at[e], dev(tm, partner),
        )

    def plane_recv(ext, e, ss, rs):
        ref = ext.at[e, own_rows, :]
        return remote(ref, ref, ss, rs.at[e], dev(tm, partner))

    def z_copy(ext, pp, up, ss, rs):
        src = ext.at[W + pp, own_rows, :]
        if up:
            e = pp - PL + W
            return remote(src, ext.at[e, own_rows, :], ss.at[0, pp], rs.at[e], dev(tm, s + 2))
        e = pp + PL + W
        return remote(src, ext.at[e, own_rows, :], ss.at[1, pp], rs.at[e], dev(tm, s - 2))

    def z_each(ext, pp, ss, rs, extra, act):
        @pl.when((pp >= PL - W) & has_up & extra)
        def _():
            act(z_copy(ext, pp, True, ss, rs))

        @pl.when((pp < W) & has_dn & extra)
        def _():
            act(z_copy(ext, pp, False, ss, rs))

    def start(c):
        c.start()

    def wait_send(c):
        c.wait_send()

    def sib_copy(e):
        ref = k.at[e, own_rows, :]
        return remote(ref, ref, k_sib.at[e], k_recv.at[e], dev(sib, s))

    always = p >= 0
    for t in range(L):
        y_copy(st_ref.at[0], b, t, b_ysend, b_recv).start()
    for t in range(L):
        b[W + h * L + t, own_rows, :] = st_ref[0, t, pl.ds(own_src, RW), :]
    for t in range(L):
        z_each(b, h * L + t, b_zsend, b_recv, always, start)

    S_EY = quarter((NY, YC), 0)
    S_EYT = quarter((YC, NY), 1)
    S_EZ = quarter((NZ, LANES), 0)
    S_EZT = quarter((LANES, NZ), 1)
    scale = 1.0 / FACTOR**3

    def cond_plane(t):
        m = mat_ref[t]
        c = jnp.zeros((NY, NZ), jnp.float32)
        for region in range(regions):
            c = jnp.where(m == region, cond_ref[region], c)
        k_slab[t] = jnp.sqrt(c)
        return c

    for lc in range(LC):
        def body(j, acc, lc=lc):
            return acc + cond_plane(lc * FACTOR + j)

        csum = lax.fori_loop(0, FACTOR, body, jnp.zeros((NY, NZ), jnp.float32))
        gath[s, LC + lc] = mm(mm(S_EYT, csum), S_EZ) * scale
    for t in range(L):
        @pl.when(par == t % 2)
        def _(t=t):
            y_copy(k_slab, k, t, k_ysend, k_recv).start()
    for t in range(L):
        k[W + h * L + t, own_rows, :] = k_slab[t, pl.ds(own_src, RW), :]
    for t in range(L):
        z_each(k, h * L + t, k_zsend, k_recv, par == t % 2, start)

    for lc in range(LC):
        ssum = st_ref[0, lc * FACTOR]
        for j in range(1, FACTOR):
            ssum = ssum + st_ref[0, lc * FACTOR + j]
        gath[s, lc] = mm(mm(S_EYT, ssum), S_EZ) * scale

    def peer_copies(ref_of, ss, rs):
        sends, recvs = [], []
        for i in range(1, S):
            to = lax.rem(s + i, S)
            fr = lax.rem(s + S - i, S)
            sends.append(remote(ref_of(s), ref_of(s), ss.at[i], rs.at[i], dev(tm, to)))
            recvs.append(remote(ref_of(fr), ref_of(fr), ss.at[i], rs.at[i], dev(tm, to)))
        return sends, recvs

    gs, gr = peer_copies(lambda j: gath.at[j], g_send, g_recv)
    for c in gs:
        c.start()

    for ext in (b, k):
        for e in range(E):
            ext[e, zero_rows, :] = jnp.zeros((RH, NZ), jnp.float32)

    @pl.when(jnp.logical_not(has_dn))
    def _():
        for ext in (b, k):
            for e in range(W):
                ext[e, own_rows, :] = jnp.zeros((RW, NZ), jnp.float32)

    @pl.when(jnp.logical_not(has_up))
    def _():
        for ext in (b, k):
            for e in range(W + PL, E):
                ext[e, own_rows, :] = jnp.zeros((RW, NZ), jnp.float32)

    for t in range(L):
        pp = (1 - h) * L + t
        plane_recv(b, W + pp, b_ysend.at[t], b_recv).wait_recv()
        z_each(b, pp, b_zsend, b_recv, always, start)
    for t in range(L):
        pp = (1 - h) * L + t

        @pl.when(par == t % 2)
        def _(t=t, pp=pp):
            plane_recv(k, W + pp, k_ysend.at[t], k_recv).wait_recv()
            z_each(k, pp, k_zsend, k_recv, always, start)
            sib_copy(W + pp).start()

    for c in gr:
        c.wait_recv()

    def coarse_of(first):
        return jnp.concatenate([gath[j, first:first + LC] for j in range(S)], axis=0)

    K = coarse_of(LC)
    shape = (XC, YC, LANES)
    row = lax.broadcasted_iota(jnp.int32, shape, 1)
    lane = lax.broadcasted_iota(jnp.int32, shape, 2)
    pad = lane >= ZC

    def moved(a):
        return (
            jnp.concatenate([a[:1], a[:-1]], axis=0),
            jnp.concatenate([a[1:], a[-1:]], axis=0),
            pltpu.roll(a, 1, 1),
            pltpu.roll(a, YC - 1, 1),
            pltpu.roll(a, 1, 2),
            pltpu.roll(a, LANES - 1, 2),
        )

    plane = lax.broadcasted_iota(jnp.int32, shape, 0)
    edges = (plane == 0, plane == XC - 1, row == 0, row == YC - 1, lane == 0, lane == ZC - 1)
    diag = jnp.ones(shape, jnp.float32)
    for i, (near, edge) in enumerate(zip(moved(K), edges)):
        coef = 0.15 * (K + jnp.where(edge, K, near))
        diag = diag + coef
        coefs[i] = jnp.where(edge | pad, 0.0, coef)
    rdiag[...] = 1.0 / diag

    halo = [(e, has_dn, (e + PL - W) % 2) for e in range(W)]
    halo += [(e, has_up, (e - PL - W) % 2) for e in range(W + PL, E)]
    for e, has, _ in halo:
        @pl.when(has)
        def _(e=e):
            plane_recv(b, e, b_ysend.at[0], b_recv).wait_recv()
    for e, has, parity in halo:
        @pl.when(has & (par == parity))
        def _(e=e):
            plane_recv(k, e, k_ysend.at[0], k_recv).wait_recv()
            sib_copy(e).start()
    for t in range(L):
        @pl.when(par != t % 2)
        def _(t=t):
            plane_recv(k, W + (1 - h) * L + t, k_ysend.at[t], k_recv).wait_recv()
    for e, has, parity in halo:
        @pl.when(has & (par != parity))
        def _(e=e):
            plane_recv(k, e, k_ysend.at[0], k_recv).wait_recv()

    lane2 = lax.broadcasted_iota(jnp.int32, (RE, NZ), 1)

    def stencil(u, e):
        c = u[e]
        w = u[e - 1] + u[e + 1] + (c + c)
        w = (w + w) + pltpu.roll(w, 1, 0) + pltpu.roll(w, RE - 1, 0)
        left = jnp.where(lane2 == 0, 0.0, pltpu.roll(w, 1, 1))
        right = jnp.where(lane2 == NZ - 1, 0.0, pltpu.roll(w, NZ - 1, 1))
        t = (w + w) + (left + right)
        return 2.4 * c - 0.0375 * t

    def inner(v):
        return jnp.sum(v[RH:RH + HY].reshape(HY // 8, 8, NZ), axis=0)

    def weight(e):
        return jnp.where((e >= W) & (e < W + PL), 1.0, 0.0)

    acc0 = jnp.zeros((8, NZ), jnp.float32)

    def moments(u0, u1, lo):
        def pass1(e, m0):
            kk = k[e]
            rr = -(kk * stencil(u0, e))
            r[e] = rr
            u1[e] = kk * rr
            return m0 + weight(e) * inner(rr * rr)

        m0 = lax.fori_loop(lo, E - lo, pass1, acc0)

        def pass2(e, m):
            kk = k[e]
            rr = r[e]
            qq = rr + kk * stencil(u1, e)
            q[e] = qq
            u0[e] = kk * qq
            return m[0] + weight(e) * inner(rr * qq), m[1] + weight(e) * inner(qq * qq)

        m1, m2 = lax.fori_loop(lo + 1, E - lo - 1, pass2, (acc0, acc0))

        def pass3(e, m3):
            return m3 + inner(u0[e] * stencil(u0, e))

        m3 = lax.fori_loop(W, W + PL, pass3, m2)
        return m0, m1, m2, m3

    def scalars(ms, g):
        rows = []
        for m in ms:
            v = jnp.sum(m, axis=0, keepdims=True)
            w = v[:, :LANES]
            for i in range(1, NZ // LANES):
                w = w + v[:, i * LANES:(i + 1) * LANES]
            rows.append(w)
        rows.append(jnp.zeros((4, LANES), jnp.float32))
        red[g, s] = jnp.concatenate(rows, axis=0)
        sends, recvs = peer_copies(lambda j: red.at[g, j], a_send.at[g], a_recv.at[g])
        for c in sends:
            c.start()
        for c in recvs:
            c.wait_recv()
        tot = red[g, 0]
        for j in range(1, S):
            tot = tot + red[g, j]
        tot = jnp.sum(tot, axis=1, keepdims=True)
        m0, m1, m2, m3 = (tot[i:i + 1] for i in range(4))
        a0 = m0 / m1
        rr1 = m0 - 2.0 * a0 * m1 + a0 * a0 * m2
        g1 = 1.0 + rr1 / m0
        curv = g1 * g1 * m1 - 2.0 * g1 * a0 * m2 + a0 * a0 * m3
        a1 = rr1 / curv
        return a0 + a1 * g1, -(a1 * a0), sends

    def first(e, _):
        ua[e] = k[e] * b[e]
        return 0

    lax.fori_loop(0, E, first, 0)
    c1, c2, sends1 = scalars(moments(ua, ub, 1), 0)

    def update(e, _):
        x = b[e] + c1 * r[e] + c2 * q[e]
        b[e] = x
        ua[e] = k[e] * x
        return 0

    for t in range(L):
        y_copy(st_ref.at[0], b, t, b_ysend, b_recv).wait_send()
    for pp in range(PL):
        z_each(b, pp, b_zsend, b_recv, always, wait_send)
    lax.fori_loop(2, E - 2, update, 0)
    c1, c2, sends2 = scalars(moments(ua, ub, 3), 1)

    rows_in = slice(RH, RH + HY)
    for pc in range(PL // FACTOR):
        def last(j, acc, pc=pc):
            i = pc * FACTOR + j
            e = W + i
            x = b[e, rows_in, :] + c1 * r[e, rows_in, :] + c2 * q[e, rows_in, :]
            xf[i] = x
            return acc + x

        xsum = lax.fori_loop(0, FACTOR, last, jnp.zeros((HY, NZ), jnp.float32))
        ey = quarter((HY // FACTOR, HY), 1)
        ce[s, pc] = mm(mm(ey, xsum), S_EZ) * scale

    cs, cr = peer_copies(lambda j: ce.at[j], c_send, c_recv)
    for c in cs:
        c.start()

    def end_copy(same):
        half = h if same else 1 - h
        to = s if same else partner
        i = 0 if same else 1
        rows = pl.ds(pl.multiple_of(h * HY, 8), HY)
        return remote(
            xf.at[pl.ds(half * L, L)], fe.at[:, rows, :], e_send.at[i], e_recv.at[i], dev(tm + 1, to)
        )

    def end_recv(same):
        src_half = h if same else 1 - h
        i = 0 if same else 1
        ref = fe.at[:, pl.ds(pl.multiple_of(src_half * HY, 8), HY), :]
        return remote(ref, ref, e_send.at[i], e_recv.at[i], dev(tm - 1, s))

    has_next = tm < T - 1

    @pl.when(has_next)
    def _():
        end_copy(False).start()
        end_copy(True).start()

    for c in cr:
        c.wait_recv()

    HC = HY // FACTOR
    for j in range(S):
        path_ref[0, (j // 2) * 2 * LC:(j // 2 + 1) * 2 * LC, (j % 2) * HC:(j % 2 + 1) * HC, :] = ce[j, :, :, :ZC]

    def relay_path():
        return remote(pout, pin, p_send.at[0], p_recv.at[0], dev(tm + 1, s))

    pout = coefs.at[6]

    def relay_d():
        return remote(dsend, din, p_send.at[1], p_recv.at[1], dev(tm + 1, s))

    def ce_full():
        blocks = []
        for j in range(0, S, 2):
            blocks.append(jnp.concatenate([ce[j], ce[j + 1]], axis=1))
        return jnp.concatenate(blocks, axis=0)

    @pl.when(tm == 0)
    def _():
        pout[...] = ce_full()
        dsend[...] = jnp.zeros((LC, YC, LANES), jnp.float32)

    @pl.when(tm > 0)
    def _():
        remote(pin, pin, p_send.at[0], p_recv.at[0], dev(tm - 1, s)).wait_recv()
        remote(din, din, p_send.at[1], p_recv.at[1], dev(tm - 1, s)).wait_recv()
        src = pin[...] - coarse_of(0)
        w = src
        for _i in range(JACOBI):
            acc = src
            for i, near in enumerate(moved(w)):
                acc = acc + coefs[i] * near
            w = acc * rdiag[...]
        pout[...] = w
        dsend[...] = coefs[6, pl.ds(s * LC, LC)]
        pth = w + ce_full()
        pout[...] = pth
        path_ref[0] = pth[:, :, :ZC]

    @pl.when(has_next)
    def _():
        relay_path().start()
        relay_d().start()

    @pl.when(tm == 0)
    def _():
        out_ref[...] = st_ref[...]

    @pl.when(tm > 0)
    def _():
        end_recv(True).wait_recv()
        end_recv(False).wait_recv()
        for lc in range(LC):
            up = mm(mm(S_EY, din[lc]), S_EZT)
            for j in range(FACTOR):
                i = lc * FACTOR + j
                out_ref[0, i] = fe[i] + up

    for t in range(L):
        @pl.when(par == t % 2)
        def _(t=t):
            y_copy(k_slab, k, t, k_ysend, k_recv).wait_send()
            sib_copy(W + (1 - h) * L + t).wait_send()
    for pp in range(PL):
        z_each(k, pp, k_zsend, k_recv, par == pp % 2, wait_send)
    for e, has, parity in halo:
        @pl.when(has & (par == parity))
        def _(e=e):
            sib_copy(e).wait_send()
    for c in gs + sends1 + sends2 + cs:
        c.wait_send()

    @pl.when(has_next)
    def _():
        end_copy(False).wait_send()
        end_copy(True).wait_send()
        relay_path().wait_send()
        relay_d().wait_send()


def local(T, S, starts, material, conductivity):
    _, L, NY, NZ = starts.shape
    E = 2 * L + 2 * W
    HY = NY // 2
    RE = HY + 2 * RH
    LC = L // FACTOR
    XC, YC, ZC = LC * S, NY // FACTOR, NZ // FACTOR
    f32 = jnp.float32
    ext = pltpu.VMEM((E, RE, NZ), f32)
    dma = pltpu.SemaphoreType.DMA
    vm = pl.BlockSpec(memory_space=pltpu.VMEM)
    return pl.pallas_call(
        functools.partial(kernel, T, S, L, NY, NZ, conductivity.shape[0]),
        out_shape=(
            jax.ShapeDtypeStruct(starts.shape, f32),
            jax.ShapeDtypeStruct((1, XC, YC, ZC), f32),
        ),
        in_specs=[pl.BlockSpec(memory_space=pltpu.SMEM), vm, vm],
        out_specs=(vm, vm),
        scratch_shapes=[
            pltpu.VMEM((L, NY, NZ), f32), ext, ext, ext, ext, ext, ext,
            pltpu.VMEM((2 * L, HY, NZ), f32), pltpu.VMEM((L, NY, NZ), f32),
            pltpu.VMEM((2, S, 8, LANES), f32),
            pltpu.VMEM((S, 2 * LC, YC, LANES), f32),
            pltpu.VMEM((S, 2 * LC, YC // 2, LANES), f32),
            pltpu.VMEM((XC, YC, LANES), f32),
            pltpu.VMEM((LC, YC, LANES), f32),
            pltpu.VMEM((LC, YC, LANES), f32),
            pltpu.VMEM((7, XC, YC, LANES), f32),
            pltpu.VMEM((XC, YC, LANES), f32),
            dma((E,)), dma((E,)), dma((L,)), dma((L,)), dma((2, 2 * L)), dma((2, 2 * L)), dma((E,)),
            dma((2, S)), dma((2, S)), dma((S,)), dma((S,)), dma((S,)), dma((S,)),
            dma((2,)), dma((2,)), dma((2,)), dma((2,)),
        ],
        compiler_params=pltpu.CompilerParams(
            collective_id=0, has_side_effects=True, vmem_limit_bytes=60 * 1024 * 1024
        ),
    )(conductivity, starts, material)


def solution(mesh):
    return jax.shard_map(
        functools.partial(local, mesh.shape["tm"], mesh.shape["space"]),
        mesh=mesh,
        in_specs=(P("tm", "space", None, None), P("space", None, None), P()),
        out_specs=(P("tm", "space", None, None), P("tm", None, None, None)),
        check_vma=False,
    )
```

time: 598 us -> 115 us (0.19)
  blocking collectives: 209 us -> 0 us
  other arithmetic: 172 us -> 0 us
  Pallas kernels: 0 us -> 108 us
  waiting for transfers between devices: 82.8 us -> 0 us
  local copies, waits for them, and re-layouts: 70.3 us -> 3.4 us
  starting transfers between devices: 45.8 us -> 0 us
  between operations: 9.37 us -> 0.65 us
    psum x6 -> x0, blocking collectives: 117 us -> none  [the longest x4 76.6 us: grid_squares(): return lax.psum(jnp.sum(resid * resid), 'space')]
    pallas_call x0 -> x1, Pallas kernels: none -> 108 us  [local(): pl.pallas_call(functools.partial(kernel, T, S, L, NY, NZ, conductivity.sh...]
    reduce_sum x12 -> x0, other arithmetic: 96.1 us -> none  [the longest x4 60.1 us: grid_curvature(): return lax.psum(jnp.sum(direction * image), 'space')]
    all_gather x3 -> x0, blocking collectives: 92.4 us -> none  [the longest x1 30.9 us: local(): coarse_end = lax.all_gather(local_end, 'space', axis=0, tiled=True)]
    ppermute x16 -> x0, waiting for transfers between devices: 82.8 us -> none  [the longest x4 37.1 us: shifted(): return lax.ppermute(x, axis, pairs)]
    mul x5 -> x0, other arithmetic: 57.2 us -> none  [operate(): scaled = root_cond * vector]
    ppermute x16 -> x0, starting transfers between devices: 45.8 us -> none  [the longest x6 30.2 us: extended(): before = lax.ppermute(last, axis, up)]
    reduce_sum x3 -> x0, local copies, waits for them, and re-layouts: 43.9 us -> none  [restrict(): return jnp.mean(blocks, axis=(1, 3, 5))]
  transfers between devices with their start and end apart: 16 -> 0, of which waited for: 12 -> 0; matrix products, arithmetic and copies ran while one was open for 7% -> 0% of each run, Pallas kernels for 0% -> 0%
where the time goes in v1:
time: 115 us; the launch traced here: 112 us
  Pallas kernels  108 us (94%)
  local copies, waits for them, and re-layouts  3.4 us (3%)
    pallas_call x1, Pallas kernels, local(): pl.pallas_call(functools.partial(kernel, T, S, L, NY, NZ, conductivity.sh...  108 us
    unnamed x4, local copies, waits for them, and re-layouts  3.4 us

profile of v1, /device:TPU:2, one launch (start us, length us, event | category | flops | bytes accessed | tf_op | source)
XLA Modules:
  0.0 112.3 jit_solution(9528457877137162549)
XLA Ops:
  0.6 108.3 %shard_map.50 = (f32[1,4,256,384]{3,2,1,0:T(8,128)}, f32[1,8,64,96]{3,2,1,0:T(8,128)}) custom-call(f32[8]{0:T(128)} %cond_ref.1, f32[1,4,256,384]{3,2,1,0:T(8,128)} %st_ref.1, s32[4,256,384]{2,1,0:T(8,128)} %mat_ref.1), custom_call_target="tpu_custom_call" | custom-call | tf_op jit(solution)/shard_map/pallas_call | solution.py:490
  108.9 0.0 copy-start
  108.9 2.7 %copy.7 = f32[1,4,256,384]{3,2,1,0:T(8,128)} copy(f32[1,4,256,384]{3,2,1,0:T(8,128)} %get-tuple-element.4) | data formatting | bytes 3145728
  111.6 0.0 copy-done
  111.6 0.7 copy.8
Async XLA Ops:
  108.9 2.7 %copy-start = (f32[1,8,64,96]{3,2,1,0:T(8,128)S(1)}, f32[1,8,64,96]{3,2,1,0:T(8,128)}, u32[]{:S(2)}) copy-start(f32[1,8,64,96]{3,2,1,0:T(8,128)} %get-tuple-element.5) | copy-start | bytes 589828

commit v2 on v1

--- a/solution.py
+++ b/solution.py
@@ -178,8 +178,6 @@
         return sends, recvs
 
     gs, gr = peer_copies(lambda j: gath.at[j], g_send, g_recv)
-    for c in gs:
-        c.start()
 
     for ext in (b, k):
         for e in range(E):
@@ -210,56 +208,12 @@
             z_each(k, pp, k_zsend, k_recv, always, start)
             sib_copy(W + pp).start()
 
-    for c in gr:
-        c.wait_recv()
-
-    def coarse_of(first):
-        return jnp.concatenate([gath[j, first:first + LC] for j in range(S)], axis=0)
-
-    K = coarse_of(LC)
-    shape = (XC, YC, LANES)
-    row = lax.broadcasted_iota(jnp.int32, shape, 1)
-    lane = lax.broadcasted_iota(jnp.int32, shape, 2)
-    pad = lane >= ZC
-
-    def moved(a):
-        return (
-            jnp.concatenate([a[:1], a[:-1]], axis=0),
-            jnp.concatenate([a[1:], a[-1:]], axis=0),
-            pltpu.roll(a, 1, 1),
-            pltpu.roll(a, YC - 1, 1),
-            pltpu.roll(a, 1, 2),
-            pltpu.roll(a, LANES - 1, 2),
-        )
-
-    plane = lax.broadcasted_iota(jnp.int32, shape, 0)
-    edges = (plane == 0, plane == XC - 1, row == 0, row == YC - 1, lane == 0, lane == ZC - 1)
-    diag = jnp.ones(shape, jnp.float32)
-    for i, (near, edge) in enumerate(zip(moved(K), edges)):
-        coef = 0.15 * (K + jnp.where(edge, K, near))
-        diag = diag + coef
-        coefs[i] = jnp.where(edge | pad, 0.0, coef)
-    rdiag[...] = 1.0 / diag
-
-    halo = [(e, has_dn, (e + PL - W) % 2) for e in range(W)]
-    halo += [(e, has_up, (e - PL - W) % 2) for e in range(W + PL, E)]
-    for e, has, _ in halo:
-        @pl.when(has)
-        def _(e=e):
-            plane_recv(b, e, b_ysend.at[0], b_recv).wait_recv()
-    for e, has, parity in halo:
-        @pl.when(has & (par == parity))
-        def _(e=e):
-            plane_recv(k, e, k_ysend.at[0], k_recv).wait_recv()
-            sib_copy(e).start()
+    for c in gs:
+        c.start()
     for t in range(L):
         @pl.when(par != t % 2)
         def _(t=t):
             plane_recv(k, W + (1 - h) * L + t, k_ysend.at[t], k_recv).wait_recv()
-    for e, has, parity in halo:
-        @pl.when(has & (par != parity))
-        def _(e=e):
-            plane_recv(k, e, k_ysend.at[0], k_recv).wait_recv()
 
     lane2 = lax.broadcasted_iota(jnp.int32, (RE, NZ), 1)
 
@@ -280,15 +234,13 @@
 
     acc0 = jnp.zeros((8, NZ), jnp.float32)
 
-    def moments(u0, u1, lo):
+    def passes(u0, u1):
         def pass1(e, m0):
             kk = k[e]
             rr = -(kk * stencil(u0, e))
             r[e] = rr
             u1[e] = kk * rr
             return m0 + weight(e) * inner(rr * rr)
-
-        m0 = lax.fori_loop(lo, E - lo, pass1, acc0)
 
         def pass2(e, m):
             kk = k[e]
@@ -298,15 +250,12 @@
             u0[e] = kk * qq
             return m[0] + weight(e) * inner(rr * qq), m[1] + weight(e) * inner(qq * qq)
 
-        m1, m2 = lax.fori_loop(lo + 1, E - lo - 1, pass2, (acc0, acc0))
-
         def pass3(e, m3):
             return m3 + inner(u0[e] * stencil(u0, e))
 
-        m3 = lax.fori_loop(W, W + PL, pass3, m2)
-        return m0, m1, m2, m3
-
-    def scalars(ms, g):
+        return pass1, pass2, pass3
+
+    def scalars(ms, g, beside=None):
         rows = []
         for m in ms:
             v = jnp.sum(m, axis=0, keepdims=True)
@@ -319,6 +268,8 @@
         sends, recvs = peer_copies(lambda j: red.at[g, j], a_send.at[g], a_recv.at[g])
         for c in sends:
             c.start()
+        if beside is not None:
+            beside()
         for c in recvs:
             c.wait_recv()
         tot = red[g, 0]
@@ -337,8 +288,35 @@
         ua[e] = k[e] * b[e]
         return 0
 
-    lax.fori_loop(0, E, first, 0)
-    c1, c2, sends1 = scalars(moments(ua, ub, 1), 0)
+    pass1, pass2, pass3 = passes(ua, ub)
+    lax.fori_loop(W, W + PL, first, 0)
+    m0 = lax.fori_loop(W + 1, W + PL - 1, pass1, acc0)
+    m12 = lax.fori_loop(W + 2, W + PL - 2, pass2, (acc0, acc0))
+
+    halo = [(e, has_dn, (e + PL - W) % 2) for e in range(W)]
+    halo += [(e, has_up, (e - PL - W) % 2) for e in range(W + PL, E)]
+    for e, has, _ in halo:
+        @pl.when(has)
+        def _(e=e):
+            plane_recv(b, e, b_ysend.at[0], b_recv).wait_recv()
+    for e, has, parity in halo:
+        @pl.when(has & (par == parity))
+        def _(e=e):
+            plane_recv(k, e, k_ysend.at[0], k_recv).wait_recv()
+            sib_copy(e).start()
+    for e, has, parity in halo:
+        @pl.when(has & (par != parity))
+        def _(e=e):
+            plane_recv(k, e, k_ysend.at[0], k_recv).wait_recv()
+
+    lax.fori_loop(0, W, first, 0)
+    lax.fori_loop(W + PL, E, first, 0)
+    m0 = lax.fori_loop(1, W + 1, pass1, m0)
+    m0 = lax.fori_loop(W + PL - 1, E - 1, pass1, m0)
+    m12 = lax.fori_loop(2, W + 2, pass2, m12)
+    m12 = lax.fori_loop(W + PL - 2, E - 2, pass2, m12)
+    m3 = lax.fori_loop(W, W + PL, pass3, m12[1])
+    c1, c2, sends1 = scalars((m0,) + m12 + (m3,), 0)
 
     def update(e, _):
         x = b[e] + c1 * r[e] + c2 * q[e]
@@ -351,7 +329,42 @@
     for pp in range(PL):
         z_each(b, pp, b_zsend, b_recv, always, wait_send)
     lax.fori_loop(2, E - 2, update, 0)
-    c1, c2, sends2 = scalars(moments(ua, ub, 3), 1)
+    def coarse_of(first):
+        return jnp.concatenate([gath[j, first:first + LC] for j in range(S)], axis=0)
+
+    def moved(a):
+        return (
+            jnp.concatenate([a[:1], a[:-1]], axis=0),
+            jnp.concatenate([a[1:], a[-1:]], axis=0),
+            pltpu.roll(a, 1, 1),
+            pltpu.roll(a, YC - 1, 1),
+            pltpu.roll(a, 1, 2),
+            pltpu.roll(a, LANES - 1, 2),
+        )
+
+    def coarse_setup():
+        for c in gr:
+            c.wait_recv()
+
+        K = coarse_of(LC)
+        shape = (XC, YC, LANES)
+        row = lax.broadcasted_iota(jnp.int32, shape, 1)
+        lane = lax.broadcasted_iota(jnp.int32, shape, 2)
+        pad = lane >= ZC
+
+        plane = lax.broadcasted_iota(jnp.int32, shape, 0)
+        edges = (plane == 0, plane == XC - 1, row == 0, row == YC - 1, lane == 0, lane == ZC - 1)
+        diag = jnp.ones(shape, jnp.float32)
+        for i, (near, edge) in enumerate(zip(moved(K), edges)):
+            coef = 0.15 * (K + jnp.where(edge, K, near))
+            diag = diag + coef
+            coefs[i] = jnp.where(edge | pad, 0.0, coef)
+        rdiag[...] = 1.0 / diag
+
+    m0 = lax.fori_loop(3, E - 3, pass1, acc0)
+    m12 = lax.fori_loop(4, E - 4, pass2, (acc0, acc0))
+    m3 = lax.fori_loop(W, W + PL, pass3, m12[1])
+    c1, c2, sends2 = scalars((m0,) + m12 + (m3,), 1, coarse_setup)
 
     rows_in = slice(RH, RH + HY)
     for pc in range(PL // FACTOR):
@@ -390,7 +403,6 @@
     @pl.when(has_next)
     def _():
         end_copy(False).start()
-        end_copy(True).start()
 
     for c in cr:
         c.wait_recv()
@@ -439,6 +451,7 @@
     def _():
         relay_path().start()
         relay_d().start()
+        end_copy(True).start()
 
     @pl.when(tm == 0)
     def _():

time: 115 us -> 106 us (0.922); the launches traced: 112 us -> 106 us
  Pallas kernels: 108 us -> 102 us
    pallas_call x1, Pallas kernels: 108 us -> 102 us  [local(): pl.pallas_call(functools.partial(kernel, T, S, L, NY, NZ, conductivity.sh...]
where the time goes in v2:
time: 106 us
  Pallas kernels  102 us (96%)
  local copies, waits for them, and re-layouts  3.4 us (3%)
    pallas_call x1, Pallas kernels, local(): pl.pallas_call(functools.partial(kernel, T, S, L, NY, NZ, conductivity.sh...  102 us
    unnamed x4, local copies, waits for them, and re-layouts  3.4 us

profile of v2, /device:TPU:2, one launch (start us, length us, event | category | flops | bytes accessed | tf_op | source)
XLA Modules:
  0.0 106.0 jit_solution(2525892550247690326)
XLA Ops:
  0.6 101.9 %shard_map.50 = (f32[1,4,256,384]{3,2,1,0:T(8,128)}, f32[1,8,64,96]{3,2,1,0:T(8,128)}) custom-call(f32[8]{0:T(128)} %cond_ref.1, f32[1,4,256,384]{3,2,1,0:T(8,128)} %st_ref.1, s32[4,256,384]{2,1,0:T(8,128)} %mat_ref.1), custom_call_target="tpu_custom_call" | custom-call | tf_op jit(solution)/shard_map/pallas_call | solution.py:503
  102.5 0.0 copy-start
  102.6 2.7 %copy.7 = f32[1,4,256,384]{3,2,1,0:T(8,128)} copy(f32[1,4,256,384]{3,2,1,0:T(8,128)} %get-tuple-element.4) | data formatting | bytes 3145728
  105.3 0.0 copy-done
  105.3 0.7 copy.8
Async XLA Ops:
  102.5 2.7 %copy-start = (f32[1,8,64,96]{3,2,1,0:T(8,128)S(1)}, f32[1,8,64,96]{3,2,1,0:T(8,128)}, u32[]{:S(2)}) copy-start(f32[1,8,64,96]{3,2,1,0:T(8,128)} %get-tuple-element.5) | copy-start | bytes 589828

commit v3 on v2

--- a/solution.py
+++ b/solution.py
@@ -215,19 +215,28 @@
         def _(t=t):
             plane_recv(k, W + (1 - h) * L + t, k_ysend.at[t], k_recv).wait_recv()
 
-    lane2 = lax.broadcasted_iota(jnp.int32, (RE, NZ), 1)
-
-    def stencil(u, e):
-        c = u[e]
-        w = u[e - 1] + u[e + 1] + (c + c)
-        w = (w + w) + pltpu.roll(w, 1, 0) + pltpu.roll(w, RE - 1, 0)
+    CH = RE // 6 if RE % 48 == 0 else RE
+    CHUNKS = range(RE // CH)
+    lane2 = lax.broadcasted_iota(jnp.int32, (CH, NZ), 1)
+
+    def part(i):
+        return slice(i * CH, (i + 1) * CH)
+
+    def stencil(u, e, i):
+        lo, hi = max(0, i * CH - 8), min(RE, (i + 1) * CH + 8)
+        rows = slice(lo, hi)
+        own = slice(i * CH - lo, i * CH - lo + CH)
+        c = u[e, rows]
+        w = u[e - 1, rows] + u[e + 1, rows] + (c + c)
+        w = ((w + w) + pltpu.roll(w, 1, 0) + pltpu.roll(w, hi - lo - 1, 0))[own]
         left = jnp.where(lane2 == 0, 0.0, pltpu.roll(w, 1, 1))
         right = jnp.where(lane2 == NZ - 1, 0.0, pltpu.roll(w, NZ - 1, 1))
         t = (w + w) + (left + right)
-        return 2.4 * c - 0.0375 * t
-
-    def inner(v):
-        return jnp.sum(v[RH:RH + HY].reshape(HY // 8, 8, NZ), axis=0)
+        return 2.4 * c[own] - 0.0375 * t
+
+    def inner(v, i):
+        v = v[max(RH - i * CH, 0):min(RH + HY - i * CH, CH)]
+        return jnp.sum(v.reshape(v.shape[0] // 8, 8, NZ), axis=0)
 
     def weight(e):
         return jnp.where((e >= W) & (e < W + PL), 1.0, 0.0)
@@ -236,22 +245,31 @@
 
     def passes(u0, u1):
         def pass1(e, m0):
-            kk = k[e]
-            rr = -(kk * stencil(u0, e))
-            r[e] = rr
-            u1[e] = kk * rr
-            return m0 + weight(e) * inner(rr * rr)
+            add = acc0
+            for i in CHUNKS:
+                kk = k[e, part(i)]
+                rr = -(kk * stencil(u0, e, i))
+                r[e, part(i)] = rr
+                u1[e, part(i)] = kk * rr
+                add = add + inner(rr * rr, i)
+            return m0 + weight(e) * add
 
         def pass2(e, m):
-            kk = k[e]
-            rr = r[e]
-            qq = rr + kk * stencil(u1, e)
-            q[e] = qq
-            u0[e] = kk * qq
-            return m[0] + weight(e) * inner(rr * qq), m[1] + weight(e) * inner(qq * qq)
+            add1 = add2 = acc0
+            for i in CHUNKS:
+                kk = k[e, part(i)]
+                rr = r[e, part(i)]
+                qq = rr + kk * stencil(u1, e, i)
+                q[e, part(i)] = qq
+                u0[e, part(i)] = kk * qq
+                add1 = add1 + inner(rr * qq, i)
+                add2 = add2 + inner(qq * qq, i)
+            return m[0] + weight(e) * add1, m[1] + weight(e) * add2
 
         def pass3(e, m3):
-            return m3 + inner(u0[e] * stencil(u0, e))
+            for i in CHUNKS:
+                m3 = m3 + inner(u0[e, part(i)] * stencil(u0, e, i), i)
+            return m3
 
         return pass1, pass2, pass3
 

time: 106 us -> 104 us (0.981)
  Pallas kernels: 102 us -> 100 us
    pallas_call x1, Pallas kernels: 102 us -> 100 us  [local(): pl.pallas_call(functools.partial(kernel, T, S, L, NY, NZ, conductivity.sh...]
where the time goes in v3:
time: 104 us
  Pallas kernels  100 us (96%)
  local copies, waits for them, and re-layouts  3.4 us (3%)
    pallas_call x1, Pallas kernels, local(): pl.pallas_call(functools.partial(kernel, T, S, L, NY, NZ, conductivity.sh...  100 us
    unnamed x4, local copies, waits for them, and re-layouts  3.4 us

profile of v3, /device:TPU:2, one launch (start us, length us, event | category | flops | bytes accessed | tf_op | source)
XLA Modules:
  0.0 104.0 jit_solution(4281709971658345912)
XLA Ops:
  0.6 100.0 %shard_map.50 = (f32[1,4,256,384]{3,2,1,0:T(8,128)}, f32[1,8,64,96]{3,2,1,0:T(8,128)}) custom-call(f32[8]{0:T(128)} %cond_ref.1, f32[1,4,256,384]{3,2,1,0:T(8,128)} %st_ref.1, s32[4,256,384]{2,1,0:T(8,128)} %mat_ref.1), custom_call_target="tpu_custom_call" | custom-call | tf_op jit(solution)/shard_map/pallas_call | solution.py:521
  100.6 0.0 copy-start
  100.6 2.7 %copy.7 = f32[1,4,256,384]{3,2,1,0:T(8,128)} copy(f32[1,4,256,384]{3,2,1,0:T(8,128)} %get-tuple-element.4) | data formatting | bytes 3145728
  103.3 0.0 copy-done
  103.3 0.7 copy.8
Async XLA Ops:
  100.6 2.7 %copy-start = (f32[1,8,64,96]{3,2,1,0:T(8,128)S(1)}, f32[1,8,64,96]{3,2,1,0:T(8,128)}, u32[]{:S(2)}) copy-start(f32[1,8,64,96]{3,2,1,0:T(8,128)} %get-tuple-element.5) | copy-start | bytes 589828
